TPU v7x, 32 devices: a whole 2x2x4 slice. The times are simulated.
32 devices in a mesh: groups: 2 (over y), fsdp: 4 (over z), tp: 2 (over x), seq: 2 (over core).
Axes of the slice: x: 2, y: 2, z: 4, core: 2. Of those that a mesh axis runs over, the one named last changes fastest.
Arguments:
- tokens: bfloat16 [12288, 5120], P(('groups', 'fsdp', 'seq'), 'tp'), parts along dimension 0, may hold values from -8 to 8
- doc_ids: int32 [12288], P(('groups', 'fsdp', 'seq')), parts along dimension 0, may hold values from 0 to 23, as said below
- block_dest: int32 [768], P(('groups', 'fsdp', 'seq')), parts along dimension 0, may hold values from 0 to 383, as said below
- norm_gain: float32 [5120], replicated, may hold values from 0.1 to 1.9
- w_query: bfloat16 [5120, 4096], P('fsdp', 'tp'), as said below
- w_key: bfloat16 [5120, 512], P('fsdp', 'tp'), as said below
- w_value: bfloat16 [5120, 512], P('fsdp', 'tp'), may hold values from -0.078125 to 0.078125
- query_gain: float32 [128], replicated, as said below
- key_gain: float32 [128], replicated, as said below
Outputs:
- attended: bfloat16 [12288, 4096], P(('groups', 'fsdp', 'seq'), 'tp'), parts along dimension 0
There are 2 independent parts, one for each index of `groups`. A program takes and returns all parts, laid end to end along the dimension named above; an argument that names none is the same for every part. Nothing has to cross between parts.
Inputs may be any that keep to these rules, and one draw needn't show every extreme that they name: `doc_ids`: trainer device d holds rows d * 768 to (d + 1) * 768 - 1; its ids are d * 3 to d * 3 + 2, in order, each on a run of rows of its own. A permutation of the blocks; owner device d holds blocks d * 48 onward, trainer device of a block is block_dest // 48; each owner device sends at most 6 blocks to one trainer device and exactly 6 to some; the j-th blocks of all owner devices go to different trainer devices. `w_query`: entries of order 5120^-1/2. `w_key`: entries of order 5120^-1/2. `query_gain`: positive gains. `key_gain`: positive gains.
All inputs are finite; a program needn't handle non-finite values.
Results may differ from a plain program's by a relative error of at most 0.0085.
Values may be sent and summed in bfloat16 or wider, within the bound.
A program may use at most 128 MiB of HBM per device.

v0:
```python
import jax
import jax.numpy as jnp
from jax import lax
from jax.sharding import PartitionSpec as P

HEAD_DIM = 128
BLOCK = 16


EPS = 1e-06
THETA = 1000000.0


def rms_rows(values, scale_gain):
    return values * lax.rsqrt(jnp.mean(values * values, axis=-1, keepdims=True) + EPS) * scale_gain


def rotate(values, position):
    half_dim = HEAD_DIM // 2
    frequency = THETA ** (-jnp.arange(half_dim, dtype=jnp.float32) * 2.0 / HEAD_DIM)
    angles = position.astype(jnp.float32)[:, None] * frequency[None, :]
    cosine = jnp.concatenate([jnp.cos(angles), jnp.cos(angles)], axis=-1)[:, None, :]
    sine_table = jnp.concatenate([jnp.sin(angles), jnp.sin(angles)], axis=-1)[:, None, :]
    first_half = values[..., :half_dim]
    second_half = values[..., half_dim:]
    turned = jnp.concatenate([-second_half, first_half], axis=-1)
    return values * cosine + turned * sine_table


def attend(query_rows, key_rows, value_rows, doc_rows):
    row_total = query_rows.shape[0]
    head_total = query_rows.shape[1]
    group_size = head_total // key_rows.shape[1]
    row_index = jnp.arange(row_total, dtype=jnp.int32)
    allowed = (doc_rows[:, None] == doc_rows[None, :]) & (row_index[None, :] <= row_index[:, None])

    def one_head(head_index):
        key_index = head_index // group_size
        query_head = lax.dynamic_index_in_dim(query_rows, head_index, 1, keepdims=False)
        key_head = lax.dynamic_index_in_dim(key_rows, key_index, 1, keepdims=False)
        value_head = lax.dynamic_index_in_dim(value_rows, key_index, 1, keepdims=False)
        scores = jnp.dot(query_head, key_head.T, preferred_element_type=jnp.float32)
        scores = jnp.where(allowed, scores, -1e30)
        row_max = jnp.max(scores, axis=1, keepdims=True)
        exponent = jnp.where(allowed, jnp.exp(scores - row_max), 0.0)
        weights = (exponent / jnp.sum(exponent, axis=1, keepdims=True)).astype(jnp.bfloat16)
        return jnp.dot(weights, value_head, preferred_element_type=jnp.float32).astype(jnp.bfloat16)

    outputs = lax.map(one_head, jnp.arange(head_total, dtype=jnp.int32))
    return jnp.transpose(outputs, (1, 0, 2)).reshape(row_total, head_total * HEAD_DIM)


def body(tokens, doc_ids, block_dest, norm_gain, w_query, w_key, w_value, query_gain, key_gain):
    peer_count = lax.axis_size(("fsdp", "seq"))
    row_count, feat_width = tokens.shape
    block_count = row_count // BLOCK
    room_size = (block_count + peer_count - 1) // peer_count
    target = block_dest // block_count
    slot_index = block_dest % block_count
    onehot = (target[:, None] == jnp.arange(peer_count, dtype=jnp.int32)[None, :]).astype(jnp.int32)
    before = jnp.cumsum(onehot, axis=0) - onehot
    rank_index = jnp.sum(before * onehot, axis=1)
    place_index = target * room_size + rank_index
    spot_index = jnp.arange(peer_count * room_size, dtype=jnp.int32)
    match_table = (place_index[None, :] == spot_index[:, None]).astype(jnp.int32)
    filled = jnp.sum(match_table, axis=1)
    picked = (
        jnp.sum(match_table * jnp.arange(block_count, dtype=jnp.int32)[None, :], axis=1)
        + (1 - filled) * block_count
    )
    labels = jnp.sum(match_table * slot_index[None, :], axis=1) + (filled - 1)
    blocks = jnp.concatenate(
        [
            tokens.reshape(block_count, BLOCK, feat_width),
            jnp.zeros((1, BLOCK, feat_width), tokens.dtype),
        ],
        axis=0,
    )
    outgoing = blocks[picked].reshape(peer_count, room_size * BLOCK, feat_width)
    arrived, slot_tags = (
        lax.all_to_all(outgoing, ("fsdp", "seq"), split_axis=0, concat_axis=0, tiled=True),
        lax.all_to_all(
            labels.reshape(peer_count, room_size),
            ("fsdp", "seq"),
            split_axis=0,
            concat_axis=0,
            tiled=True,
        ),
    )
    slot_tags = slot_tags.reshape(-1)
    order_table = (slot_tags[None, :] == jnp.arange(block_count, dtype=jnp.int32)[:, None]).astype(
        jnp.int32
    )
    source = jnp.sum(order_table * spot_index[None, :], axis=1)
    local_rows = arrived.reshape(peer_count * room_size, BLOCK, feat_width)[source].reshape(
        row_count, feat_width
    )
    features = lax.all_gather(local_rows, "tp", axis=1, tiled=True)
    normed = rms_rows(features.astype(jnp.float32), norm_gain).astype(jnp.bfloat16)
    query_cols = w_query.shape[1]
    pieces = (
        lax.all_gather(w_query, "fsdp", axis=0, tiled=True),
        lax.all_gather(w_key, "fsdp", axis=0, tiled=True),
        lax.all_gather(w_value, "fsdp", axis=0, tiled=True),
    )
    query_raw, key_raw, value_raw = tuple(
        (
            jnp.dot(normed, weight_piece, preferred_element_type=jnp.float32)
            for weight_piece in pieces
        )
    )
    query_raw = query_raw.reshape(row_count, -1, HEAD_DIM)
    key_raw = key_raw.reshape(row_count, -1, HEAD_DIM)
    value_rows = value_raw.astype(jnp.bfloat16).reshape(row_count, -1, HEAD_DIM)
    position = jnp.arange(row_count, dtype=jnp.int32) - jnp.searchsorted(
        doc_ids, doc_ids, side="left"
    )
    query_rows = (rotate(rms_rows(query_raw, query_gain), position) * HEAD_DIM ** (-0.5)).astype(
        jnp.bfloat16
    )
    key_rows = rotate(rms_rows(key_raw, key_gain), position).astype(jnp.bfloat16)
    result = attend(query_rows, key_rows, value_rows, doc_ids)
    padded = jnp.concatenate(
        [
            result.reshape(block_count, BLOCK, query_cols),
            jnp.zeros((1, BLOCK, query_cols), result.dtype),
        ],
        axis=0,
    )
    back_index = jnp.where(slot_tags < 0, block_count, slot_tags)
    outgoing_back = padded[back_index].reshape(peer_count, room_size * BLOCK, query_cols)
    returned = lax.all_to_all(
        outgoing_back, ("fsdp", "seq"), split_axis=0, concat_axis=0, tiled=True
    )
    owner_rows = returned.reshape(peer_count * room_size, BLOCK, query_cols)[place_index].reshape(
        row_count, query_cols
    )
    return owner_rows


def solution(mesh):
    in_specs = (
        P(("groups", "fsdp", "seq"), "tp"),
        P(("groups", "fsdp", "seq")),
        P(("groups", "fsdp", "seq")),
        P(),
        P("fsdp", "tp"),
        P("fsdp", "tp"),
        P("fsdp", "tp"),
        P(),
        P(),
    )
    out_specs = P(("groups", "fsdp", "seq"), "tp")
    return jax.shard_map(body, mesh=mesh, in_specs=in_specs, out_specs=out_specs, check_vma=False)
```

profile of v0, /device:TPU:0, one launch (start us, length us, event | category | flops | bytes accessed | tf_op | source)
XLA Modules:
  0.0 965.6 jit_solution(3581551773313113424)
XLA Ops:
  8.4 6.3 all-to-all-start.1
  14.7 4.4 concatenate.20
  19.1 4.9 gather_fusion.1
  24.1 5.1 all-to-all-start
  30.6 87.1 %all-to-all-done = bf16[8,96,2560]{2,1,0:T(8,128)(2,1)} async-done(((bf16[8,96,2560]{2,1,0:T(8,128)(2,1)}), bf16[8,96,2560]{2,1,0:T(8,128)(2,1)}, u32[]{:S(2)}, u32[]{:S(2)}) %all-to-all-start) | async-done | bytes 3932192 | tf_op jit(solution)/shard_map/all_to_all | solution.py:81
  117.7 4.9 gather_fusion.2
  124.8 32.8 %while.39 = (s32[]{:T(128)}, u32[768]{0:T(1024)S(1)}, u32[768]{0:T(1024)S(1)}, s32[768]{0:T(1024)S(1)}, s32[]{:T(128)}, /*index=5*/s32[]{:T(128)}, s32[]{}) while((s32[]{:T(128)}, u32[768]{0:T(1024)S(1)}, u32[768]{0:T(1024)S(1)}, s32[768]{0:T(1024)S(1)}, s32[]{:T(128)}, /*index=5*/s32[]{:T(128)}, s32[]{}) %tuple.91), condition=%wide.region_9.10_spmd.clone, body=%wide.region_8.9_spmd.clone.sunk | while | flops 14852 | bytes 57957 | solution.py:115
  124.8 3.2 gather_fusion
  159.5 60.3 %all-gather.5.cloned.1.call-done = bf16[768,5120]{1,0:T(8,128)(2,1)} async-done(((bf16[768,2560]{1,0:T(8,128)(2,1)}), bf16[768,5120]{1,0:T(8,128)(2,1)}) %all-gather.5.cloned.1.call-update) | async-done | bytes 7864336 | tf_op jit(solution)/shard_map/all_gather | solution.py:98
  219.8 4.8 fusion.21
  224.6 51.6 %all-gather.9.cloned.1.call-done = bf16[5120,256]{1,0:T(8,128)(2,1)} async-done(((bf16[1280,256]{1,0:T(8,128)(2,1)}), bf16[5120,256]{1,0:T(8,128)(2,1)}) %all-gather.9.cloned.1.call-update) | async-done | bytes 2621456 | tf_op jit(solution)/shard_map/all_gather | solution.py:103
  276.2 6.6 multiply_reduce_fusion.1
  285.0 46.4 %all-gather.11.cloned.1.call-done = bf16[5120,256]{1,0:T(8,128)(2,1)} async-done(((bf16[1280,256]{1,0:T(8,128)(2,1)}), bf16[5120,256]{1,0:T(8,128)(2,1)}) %all-gather.11.cloned.1.call-update) | async-done | bytes 2621456 | tf_op jit(solution)/shard_map/all_gather | solution.py:104
  331.4 7.4 convolution_convert_fusion
  338.8 349.7 %all-gather.7.cloned.1.call-done = bf16[5120,2048]{1,0:T(8,128)(2,1)} async-done(((bf16[1280,2048]{1,0:T(8,128)(2,1)}), bf16[5120,2048]{1,0:T(8,128)(2,1)}) %all-gather.7.cloned.1.call-update) | async-done | bytes 20971536 | tf_op jit(solution)/shard_map/all_gather | solution.py:102
  688.5 20.9 %fusion.37 = f32[768,2048]{1,0:T(8,128)S(1)} fusion(bf16[5120,2048]{1,0:T(8,128)(2,1)} %all-gather.7.cloned.1.call-done, bf16[768,5120]{1,0:T(8,128)(2,1)} %all-gather.5.cloned.1.call-done, f32[5120]{0:T(1024)S(1)} %copy-done.6, f32[768]{0:T(1024)S(1)} %add_rsqrt_fusion.2), kind=kOutput, calls=%fused_computation.87 | convolution fusion | flops 16121856000 | bytes 35150848 | tf_op jit(solution)/shard_map/dot_general | solution.py:108
  714.6 7.6 fusion.24
  722.2 11.1 %slice_negate_fusion = (f32[768,16,64]{2,0,1:T(8,128)}, f32[768,16,64]{2,0,1:T(8,128)}) fusion(f32[768,16,128]{2,0,1:T(8,128)} %fusion.24), kind=kLoop, calls=%fused_computation.39 | loop fusion | flops 786432 | bytes 12582912 | tf_op jit(solution)/shard_map/neg | solution.py:26
  733.3 8.2 fusion.27
  741.5 128.0 %while.38 = (s32[]{:T(128)}, bf16[16,768,128]{2,1,0:T(8,128)(2,1)}, s32[16]{0:T(128)S(1)}, bf16[768,16,128]{2,0,1:T(8,128)(2,1)}, bf16[768,2,128]{2,0,1:T(8,128)...) while((s32[]{:T(128)}, bf16[16,768,128]{2,1,0:T(8,128)(2,1)}, ...), condition=%wide.region_14.15_spmd.clone, body=%wide.region_11.14_spmd.clone.sunk | while | flops 313883136 | bytes 9474954 | solution.py:49
  869.5 3.9 copy.33
  873.4 3.3 reshape_reshape.3
  881.4 3.7 all-to-all-start.2
  885.1 71.4 %all-to-all-done.2 = bf16[8,96,2048]{2,1,0:T(8,128)(2,1)S(1)} async-done(((bf16[8,96,2048]{2,1,0:T(8,128)(2,1)}), bf16[8,96,2048]{2,1,0:T(8,128)(2,1)S(1)}, u32[]{:S(2)}, u32[]{:S(2)}) %all-to-all-start.2) | async-done | bytes 3145760 | tf_op jit(solution)/shard_map/all_to_all | solution.py:132
  (224 shorter events, 118.7 us)
Async XLA Ops:
  8.4 15.7 %all-to-all-start.1 = ((s32[8,1,6]{2,1,0:T(1,128)}), s32[8,1,6]{2,1,0:T(1,128)S(1)}, u32[]{:S(2)}, u32[]{:S(2)}) async-start(s32[8,1,6]{2,1,0:T(1,128)} %bitcast.5), calls=%async_computation.1 | async-start | bytes 8192 | tf_op jit(solution)/shard_map/all_to_all | solution.py:82
  24.1 93.6 %all-to-all-start = ((bf16[8,96,2560]{2,1,0:T(8,128)(2,1)}), bf16[8,96,2560]{2,1,0:T(8,128)(2,1)}, u32[]{:S(2)}, u32[]{:S(2)}) async-start(bf16[8,96,2560]{2,1,0:T(8,128)(2,1)} %bitcast.73), calls=%async_computation | async-start | bytes 7864320 | tf_op jit(solution)/shard_map/all_to_all | solution.py:81
  29.2 190.6 %all-gather.5.cloned.1.call-start = ((), (), s32[]{:S(2)}) async-start(), calls=%async_computation.3 | async-start | bytes 11796480 | tf_op jit(solution)/shard_map/all_gather | solution.py:98
  122.6 153.6 %all-gather.9.cloned.1.call-start = ((), (), s32[]{:S(2)}) async-start(), calls=%async_computation.5 | async-start | bytes 3276800 | tf_op jit(solution)/shard_map/all_gather | solution.py:103
  123.4 208.0 %all-gather.11.cloned.1.call-start = ((), (), s32[]{:S(2)}) async-start(), calls=%async_computation.6 | async-start | bytes 3276800 | tf_op jit(solution)/shard_map/all_gather | solution.py:104
  124.1 564.4 %all-gather.7.cloned.1.call-start = ((), (), s32[]{:S(2)}) async-start(), calls=%async_computation.4 | async-start | bytes 26214400 | tf_op jit(solution)/shard_map/all_gather | solution.py:102
  159.3 124.4 %copy-start.2 = (f32[768,128]{1,0:T(8,128)}, f32[768,128]{1,0:T(8,128)S(1)}, u32[]{:S(2)}) copy-start(f32[768,128]{1,0:T(8,128)S(1)} %get-tuple-element.273) | copy-start | bytes 1179652
  159.4 116.8 %copy-start.6 = (f32[5120]{0:T(1024)S(1)}, f32[5120]{0:T(1024)}, u32[]{:S(2)}) copy-start(f32[5120]{0:T(1024)} %param.16) | copy-start | bytes 61444
  224.6 58.5 %copy-start.4 = (f32[128]{0:T(128)S(1)}, f32[128]{0:T(128)}, u32[]{:S(2)}) copy-start(f32[128]{0:T(128)} %param.21) | copy-start | bytes 1540
  714.6 18.6 %slice-start = ((s8[6291456]{0:T(1024)(128)(4,1)}), s8[4194304]{0:T(1024)(128)(4,1)S(1)}, s32[]{:S(2)}) async-start(s8[6291456]{0:T(1024)(128)(4,1)} %bitcast.69), calls=%async_computation.7 | async-start | bytes 8388608
  722.2 11.1 %slice-start.1 = ((s8[6291456]{0:T(1024)(128)(4,1)}), s8[2097152]{0:T(1024)(128)(4,1)S(1)}, s32[]{:S(2)}) async-start(s8[6291456]{0:T(1024)(128)(4,1)} %bitcast.69), calls=%async_computation.8 | async-start | bytes 4194304
  741.5 6.4 copy-start.7
  749.5 6.4 copy-start.7
  757.5 6.4 copy-start.7
  765.5 6.4 copy-start.7
  773.5 6.4 copy-start.7
  781.5 6.4 copy-start.7
  789.5 6.4 copy-start.7
  797.5 6.4 copy-start.7
  805.5 6.4 copy-start.7
  813.5 6.4 copy-start.7
  821.5 6.4 copy-start.7
  829.5 6.4 copy-start.7
  881.4 75.1 %all-to-all-start.2 = ((bf16[8,96,2048]{2,1,0:T(8,128)(2,1)}), bf16[8,96,2048]{2,1,0:T(8,128)(2,1)S(1)}, u32[]{:S(2)}, u32[]{:S(2)}) async-start(bf16[8,96,2048]{2,1,0:T(8,128)(2,1)} %bitcast.75), calls=%async_computation.2 | async-start | bytes 6291456 | tf_op jit(solution)/shard_map/all_to_all | solution.py:132
  (8 other events, 33.6 us)
Sparse Core Ops, SparseCore 0:
  122.7 96.9 all-gather.4
  221.4 54.8 all-gather.8
  277.8 53.5 all-gather.10
  332.8 355.6 all-gather.6
where the time goes:
time: 967 us; the launch traced here: 966 us
  waiting for transfers between devices  668 us (69%)
  matrix products  85.1 us (9%)
  local copies, waits for them, and re-layouts  75.2 us (8%)
  loops' own time  60.6 us (6%)
  other arithmetic  47.6 us (5%)
  starting transfers between devices  15.2 us (2%)
  between operations  13.4 us (1%)
    all_gather x1, waiting for transfers between devices, body(): lax.all_gather(w_query, 'fsdp', axis=0, tiled=True)  350 us
    all_to_all x1, waiting for transfers between devices, body(): lax.all_to_all(outgoing, ('fsdp', 'seq'), split_axis=0, concat_axis=0, ti...  87.1 us
    all_to_all x1, waiting for transfers between devices, body(): lax.all_to_all(outgoing_back, ('fsdp', 'seq'), split_axis=0, concat_axis=...  71.4 us
    all_gather x1, waiting for transfers between devices, body(): features = lax.all_gather(local_rows, 'tp', axis=1, tiled=True)  60.3 us
    another operation x1, loops' own time, attend(): outputs = lax.map(one_head, jnp.arange(head_total, dtype=jnp.int32))  60 us
    all_gather x1, waiting for transfers between devices, body(): lax.all_gather(w_key, 'fsdp', axis=0, tiled=True)  51.6 us
    all_gather x1, waiting for transfers between devices, body(): lax.all_gather(w_value, 'fsdp', axis=0, tiled=True)  46.4 us
    dot_general x3, matrix products, body(): jnp.dot(normed, weight_piece, preferred_element_type=jnp.float32)  34.9 us
  transfers between devices with their start and end apart: 7, of which 6 were waited for; matrix products, arithmetic and copies ran while one was open for 7% of the time, Pallas kernels for 0%

commit v1 on v0

v1 whole, which is shorter than its diff:
```python
import functools

import jax
import jax.numpy as jnp
from jax import lax
from jax.experimental import pallas as pl
from jax.experimental.pallas import tpu as pltpu
from jax.sharding import PartitionSpec as P

HEAD_DIM = 128
BLOCK = 16
GROUP = 8
ROWS = 256
EPS = 1e-06
THETA = 1000000.0
MESH = pl.DeviceIdType.MESH


def kernel(
    sizes, x_ref, wq_ref, wk_ref, wv_ref, ngain_ref, qgain_ref, kgain_ref, cos_ref, sin_ref, bias_ref,
    ret_ref, w_buf, x_buf, s_buf, r_buf, o_buf,
    own_sem, xl_sem, xs_sem, xr_sem, zs_sem, zr_sem, ys_sem, yr_sem, cs_sem, cr_sem,
    dl_sem, ds_sem, dr_sem, bl_sem, bs_sem, br_sem,
):
    n, tps, cores = sizes
    y, z, t, c = (lax.axis_index(a) for a in ("groups", "fsdp", "tp", "seq"))
    chunks, depth, width = w_buf.shape
    shard = depth // n
    quarter = shard // 4
    rows = x_ref.shape[0]
    feat = x_ref.shape[1]
    peers = n * cores
    slab = rows // peers
    half = width // 2
    me = z * cores + c

    own_rows = pl.ds(pl.multiple_of(z * shard, 16), shard)
    own_copies = [
        [
            pltpu.make_async_copy(wk_ref, w_buf.at[0, own_rows, pl.ds(0, half)], own_sem.at[0]),
            pltpu.make_async_copy(wv_ref, w_buf.at[0, own_rows, pl.ds(half, half)], own_sem.at[chunks]),
        ]
    ]
    for j in range(1, chunks):
        own_copies.append(
            [pltpu.make_async_copy(wq_ref.at[:, pl.ds((j - 1) * width, width)], w_buf.at[j, own_rows, :], own_sem.at[j])]
        )
    for copies in own_copies:
        for copy in copies:
            copy.start()
    x_local = pltpu.make_async_copy(x_ref, x_buf.at[t], xl_sem)
    x_local.start()

    barrier = pltpu.get_barrier_semaphore()

    def peer_of(k):
        p = lax.rem(me + k, peers)
        return p, {"fsdp": p // cores, "seq": lax.rem(p, cores)}

    @pl.loop(1, peers)
    def _(k):
        _, dev = peer_of(k)
        pl.semaphore_signal(barrier, inc=1, device_id=dev, device_id_type=MESH)

    for k in range(1, tps):
        pl.semaphore_signal(barrier, inc=1, device_id={"tp": lax.rem(t + k, tps)}, device_id_type=MESH)
    pl.semaphore_signal(barrier, inc=1, device_id={"groups": 1 - y}, device_id_type=MESH)
    pl.semaphore_wait(barrier, peers - 1 + tps - 1 + 1)

    x_copies = [
        pltpu.make_async_remote_copy(
            src_ref=x_ref, dst_ref=x_buf.at[t], send_sem=xs_sem.at[k - 1], recv_sem=xr_sem,
            device_id={"tp": lax.rem(t + k, tps)}, device_id_type=MESH,
        )
        for k in range(1, tps)
    ]
    for copy in x_copies:
        copy.start()

    def piece(j, s, q):
        return w_buf.at[j, pl.ds(pl.multiple_of(s * shard + q * quarter, 16), quarter), :]

    mine = y * 2 + c
    other = (1 - y) * 2 + c

    def z_copy(j, s, way):
        ref = piece(j, s, mine)
        return pltpu.make_async_remote_copy(
            src_ref=ref, dst_ref=ref, send_sem=zs_sem.at[way, j, s], recv_sem=zr_sem.at[j, s],
            device_id={"fsdp": z + 1 if way == 0 else z - 1}, device_id_type=MESH,
        )

    def y_copy(j, s):
        ref = piece(j, s, mine)
        return pltpu.make_async_remote_copy(
            src_ref=ref, dst_ref=ref, send_sem=ys_sem.at[j], recv_sem=yr_sem.at[j, s],
            device_id={"groups": 1 - y}, device_id_type=MESH,
        )

    def c_copy(j, s, q):
        ref = piece(j, s, q)
        return pltpu.make_async_remote_copy(
            src_ref=ref, dst_ref=ref, send_sem=cs_sem.at[j], recv_sem=cr_sem.at[j],
            device_id={"seq": 1 - c}, device_id_type=MESH,
        )

    for j in range(chunks):
        for copy in own_copies[j]:
            copy.wait()

        @pl.when(z + 1 < n)
        def _():
            z_copy(j, z, 0).start()

        @pl.when(z >= 1)
        def _():
            z_copy(j, z, 1).start()

    def z_arrival(j, s, way, go_on):
        ref = piece(j, s, mine)
        pltpu.make_async_copy(ref, ref, zr_sem.at[j, s]).wait()

        @pl.when(go_on)
        def _():
            z_copy(j, s, way).start()

        y_copy(j, s).start()
        c_copy(j, s, mine).start()

    def y_arrival(j, s):
        ref = piece(j, s, other)
        pltpu.make_async_copy(ref, ref, yr_sem.at[j, s]).wait()
        c_copy(j, s, other).start()

    def z_step(j, step):
        @pl.when(z - step >= 0)
        def _():
            z_arrival(j, z - step, 0, z + 1 < n)

        @pl.when(z + step < n)
        def _():
            z_arrival(j, z + step, 1, z >= 1)

    def y_step(j, step):
        @pl.when(z - step >= 0)
        def _():
            y_arrival(j, z - step)

        @pl.when(z + step < n)
        def _():
            y_arrival(j, z + step)

    def weights(j):
        z_step(j, 1)
        if j > 0:
            y_step(j - 1, n - 1)

        @pl.loop(2, n)
        def _(step):
            z_step(j, step)
            y_step(j, step - 1)

    def normalise():
        x_local.wait()
        for copy in x_copies:
            copy.wait_send()
        arrived = x_buf.at[pl.ds(0, tps - 1)]
        pltpu.make_async_copy(arrived, arrived, xr_sem).wait()

        @pl.loop(0, rows // 32)
        def _(i):
            r = pl.ds(pl.multiple_of(i * 32, 32), 32)
            total = jnp.zeros((32, 1), jnp.float32)
            for k in range(tps):
                part = x_buf[k, r, :].astype(jnp.float32)
                total = total + jnp.sum(part * part, axis=-1, keepdims=True)
            scale = lax.rsqrt(total * (1.0 / depth) + EPS)
            for k in range(tps):
                part = x_buf[k, r, :].astype(jnp.float32)
                gain = ngain_ref[:, k * feat:(k + 1) * feat]
                x_buf[k, r, :] = (part * scale * gain).astype(jnp.bfloat16)

    def head_out(values, gain, r, scale):
        values = values * lax.rsqrt(jnp.mean(values * values, axis=-1, keepdims=True) + EPS) * gain
        values = values * cos_ref[r, :] + pltpu.roll(values, HEAD_DIM // 2, 1) * sin_ref[r, :]
        if scale is not None:
            values = values * scale
        return values.astype(jnp.bfloat16)

    def project(j):
        @pl.loop(0, rows // ROWS)
        def _(i):
            r = pl.ds(pl.multiple_of(i * ROWS, ROWS), ROWS)
            total = None
            for k in range(tps):
                part = jnp.dot(
                    x_buf[k, r, :], w_buf[j, k * feat:(k + 1) * feat, :], preferred_element_type=jnp.float32
                )
                total = part if total is None else total + part
            for h in range(width // HEAD_DIM):
                cols = slice(h * HEAD_DIM, (h + 1) * HEAD_DIM)
                values = total[:, cols]
                if j > 0:
                    done = head_out(values, qgain_ref[...], r, HEAD_DIM ** (-0.5))
                elif h * HEAD_DIM < half:
                    done = head_out(values, kgain_ref[...], r, None)
                else:
                    done = values.astype(jnp.bfloat16)
                s_buf[j, r, cols] = done

    def slab_of(p):
        return pl.ds(pl.multiple_of(p * slab, 16), slab)

    def dispatch_local(j):
        return pltpu.make_async_copy(s_buf.at[j, slab_of(me), :], r_buf.at[j, slab_of(me), :], dl_sem.at[j])

    def dispatch(j):
        @pl.loop(1, peers)
        def _(k):
            p, dev = peer_of(k)
            pltpu.make_async_remote_copy(
                src_ref=s_buf.at[j, slab_of(p), :], dst_ref=r_buf.at[j, slab_of(me), :],
                send_sem=ds_sem.at[j], recv_sem=dr_sem.at[j], device_id=dev, device_id_type=MESH,
            ).start()

        dispatch_local(j).start()

    def dispatched(j):
        dispatch_local(j).wait()
        ref = r_buf.at[j, pl.ds(0, (peers - 1) * slab), :]
        pltpu.make_async_copy(ref, ref, dr_sem.at[j]).wait()

    def attend(j):
        kv = ((j - 1) * width) // (GROUP * HEAD_DIM)

        @pl.loop(0, rows // ROWS)
        def _(i):
            r = pl.ds(pl.multiple_of(i * ROWS, ROWS), ROWS)
            key = r_buf[0, :, kv * HEAD_DIM:(kv + 1) * HEAD_DIM]
            value = r_buf[0, :, half + kv * HEAD_DIM:half + (kv + 1) * HEAD_DIM]
            for h in range(width // HEAD_DIM):
                cols = slice(h * HEAD_DIM, (h + 1) * HEAD_DIM)
                scores = lax.dot_general(
                    r_buf[j, r, cols], key, (((1,), (1,)), ((), ())), preferred_element_type=jnp.float32
                )
                scores = scores + bias_ref[r, :].astype(jnp.float32)
                exponent = jnp.exp(scores - jnp.max(scores, axis=1, keepdims=True))
                total = jnp.sum(exponent, axis=1, keepdims=True)
                out = jnp.dot(exponent.astype(jnp.bfloat16), value, preferred_element_type=jnp.float32)
                o_buf[j - 1, r, cols] = (out / total).astype(jnp.bfloat16)

    def back_local(j):
        return pltpu.make_async_copy(
            o_buf.at[j - 1, slab_of(me), :], ret_ref.at[slab_of(me), pl.ds((j - 1) * width, width)], bl_sem.at[j - 1]
        )

    def back(j):
        @pl.loop(1, peers)
        def _(k):
            p, dev = peer_of(k)
            pltpu.make_async_remote_copy(
                src_ref=o_buf.at[j - 1, slab_of(p), :],
                dst_ref=ret_ref.at[slab_of(me), pl.ds((j - 1) * width, width)],
                send_sem=bs_sem.at[j - 1], recv_sem=br_sem.at[j - 1], device_id=dev, device_id_type=MESH,
            ).start()

        back_local(j).start()

    def ready(j):
        ref = w_buf.at[j, pl.ds(0, 2 * (n - 1) * quarter), :]
        pltpu.make_async_copy(ref, ref, cr_sem.at[j]).wait()

    def serve(j):
        if j == 1:
            dispatched(0)
        dispatched(j)
        attend(j)
        back(j)

    for j in range(chunks + 1):
        if j < chunks:
            weights(j)
        else:
            y_step(chunks - 1, n - 1)
        if j == 1:
            normalise()
        if j >= 1:
            ready(j - 1)
            project(j - 1)
            dispatch(j - 1)
        if j >= 4:
            serve(j - 3)
    for j in range(chunks - 2, chunks):
        serve(j)

    for j in range(1, chunks):
        back_local(j).wait()
        ref = ret_ref.at[pl.ds(0, (peers - 1) * slab), pl.ds((j - 1) * width, width)]
        pltpu.make_async_copy(ref, ref, br_sem.at[j - 1]).wait()
        ref = o_buf.at[j - 1, pl.ds(0, (peers - 1) * slab), :]
        pltpu.make_async_copy(ref, ref, bs_sem.at[j - 1]).wait()
    for j in range(chunks):
        ref = s_buf.at[j, pl.ds(0, (peers - 1) * slab), :]
        pltpu.make_async_copy(ref, ref, ds_sem.at[j]).wait()
        ref = w_buf.at[j, pl.ds(0, (n - 1) * quarter), :]
        pltpu.make_async_copy(ref, ref, ys_sem.at[j]).wait()
        ref = w_buf.at[j, pl.ds(0, 2 * (n - 1) * quarter), :]
        pltpu.make_async_copy(ref, ref, cs_sem.at[j]).wait()

        @pl.loop(0, n)
        def _(s):
            ref = piece(j, s, mine)

            @pl.when((s <= z) & (z + 1 < n))
            def _():
                pltpu.make_async_copy(ref, ref, zs_sem.at[0, j, s]).wait()

            @pl.when((s >= z) & (z >= 1))
            def _():
                pltpu.make_async_copy(ref, ref, zs_sem.at[1, j, s]).wait()


def body(tokens, doc_ids, block_dest, norm_gain, w_query, w_key, w_value, query_gain, key_gain):
    n = lax.axis_size("fsdp")
    tps = lax.axis_size("tp")
    cores = lax.axis_size("seq")
    peers = n * cores
    row_count, feat = tokens.shape
    block_count = row_count // BLOCK
    room = (block_count + peers - 1) // peers
    spots = peers * room
    rows = spots * BLOCK
    width = 2 * w_key.shape[1]
    query_cols = w_query.shape[1]
    nq = query_cols // width
    chunks = nq + 1
    depth = w_key.shape[0] * n

    target = block_dest // block_count
    slot = block_dest % block_count
    onehot = (target[:, None] == jnp.arange(peers, dtype=jnp.int32)[None, :]).astype(jnp.int32)
    before = jnp.cumsum(onehot, axis=0) - onehot
    place = target * room + jnp.sum(before * onehot, axis=1)
    spot = jnp.arange(spots, dtype=jnp.int32)
    match = (place[None, :] == spot[:, None]).astype(jnp.int32)
    filled = jnp.sum(match, axis=1)
    picked = jnp.sum(match * jnp.arange(block_count, dtype=jnp.int32)[None, :], axis=1)
    labels = jnp.sum(match * slot[None, :], axis=1) + (filled - 1)
    packed = tokens.reshape(block_count, BLOCK, feat)[picked].reshape(rows, feat)

    row_index = jnp.arange(row_count, dtype=jnp.int32)
    first = jnp.sum((doc_ids[None, :] < doc_ids[:, None]).astype(jnp.int32), axis=1)
    position = row_index - first
    notes = jnp.concatenate(
        [jnp.broadcast_to(position[None, :], (peers, row_count)), labels.reshape(peers, room)], axis=1
    )
    notes = lax.all_to_all(notes, ("fsdp", "seq"), split_axis=0, concat_axis=0, tiled=True)
    positions = notes[:, :row_count].reshape(peers, block_count, BLOCK)
    tags = notes[:, row_count:].reshape(spots)
    hit = (labels.reshape(peers, room)[:, :, None] == jnp.arange(block_count, dtype=jnp.int32)).astype(jnp.int32)
    packed_position = jnp.sum(hit[:, :, :, None] * positions[:, None, :, :], axis=2).reshape(rows)
    frequency = THETA ** (-jnp.arange(HEAD_DIM // 2, dtype=jnp.float32) * 2.0 / HEAD_DIM)
    angles = packed_position.astype(jnp.float32)[:, None] * frequency[None, :]
    cosine, sine = jnp.cos(angles), jnp.sin(angles)
    cosine = jnp.concatenate([cosine, cosine], axis=1)
    sine = jnp.concatenate([-sine, sine], axis=1)
    seat = (tags[:, None] == jnp.arange(block_count, dtype=jnp.int32)[None, :]).astype(jnp.int32)
    docs = jnp.sum(seat[:, :, None] * (doc_ids.reshape(block_count, BLOCK) + 1)[None], axis=1).reshape(rows)
    order = (tags[:, None] * BLOCK + jnp.arange(BLOCK, dtype=jnp.int32)[None, :]).reshape(rows)
    allowed = (docs[:, None] == docs[None, :]) & (order[None, :] <= order[:, None])
    bias = jnp.where(allowed, 0.0, -1e30).astype(jnp.bfloat16)

    hbm = pl.BlockSpec(memory_space=pl.ANY)
    vmem = pl.BlockSpec(memory_space=pltpu.VMEM)
    dma = pltpu.SemaphoreType.DMA
    returned = pl.pallas_call(
        functools.partial(kernel, (n, tps, cores)),
        out_shape=jax.ShapeDtypeStruct((rows, query_cols), jnp.bfloat16),
        in_specs=[hbm] * 4 + [vmem] * 6,
        out_specs=hbm,
        scratch_shapes=[
            pltpu.VMEM((chunks, depth, width), jnp.bfloat16),
            pltpu.VMEM((tps, rows, feat), jnp.bfloat16),
            pltpu.VMEM((chunks, rows, width), jnp.bfloat16),
            pltpu.VMEM((chunks, rows, width), jnp.bfloat16),
            pltpu.VMEM((nq, rows, width), jnp.bfloat16),
            dma((chunks + 1,)), dma, dma((tps - 1,)), dma,
            dma((2, chunks, n)), dma((chunks, n)),
            dma((chunks,)), dma((chunks, n)),
            dma((chunks,)), dma((chunks,)),
            dma((chunks,)), dma((chunks,)), dma((chunks,)),
            dma((nq,)), dma((nq,)), dma((nq,)),
        ],
        compiler_params=pltpu.CompilerParams(
            collective_id=0, has_side_effects=True, vmem_limit_bytes=62 * 1024 * 1024
        ),
        cost_estimate=pl.CostEstimate(
            flops=2 * rows * depth * width * chunks + 4 * rows * rows * query_cols,
            bytes_accessed=2 * depth * width * chunks, transcendentals=rows * rows * query_cols // HEAD_DIM,
        ),
    )(
        packed, w_query, w_key, w_value, norm_gain[None, :], query_gain[None, :], key_gain[None, :],
        cosine, sine, bias,
    )
    return returned.reshape(spots, BLOCK, query_cols)[place].reshape(row_count, query_cols)


def solution(mesh):
    in_specs = (
        P(("groups", "fsdp", "seq"), "tp"),
        P(("groups", "fsdp", "seq")),
        P(("groups", "fsdp", "seq")),
        P(),
        P("fsdp", "tp"),
        P("fsdp", "tp"),
        P("fsdp", "tp"),
        P(),
        P(),
    )
    out_specs = P(("groups", "fsdp", "seq"), "tp")
    return jax.shard_map(body, mesh=mesh, in_specs=in_specs, out_specs=out_specs, check_vma=False)
```

time: 967 us -> 343 us (0.35)
  waiting for transfers between devices: 668 us -> 0.01 us
  Pallas kernels: 0 us -> 312 us
  matrix products: 85.1 us -> 0 us
  local copies, waits for them, and re-layouts: 75.2 us -> 10.7 us
  loops' own time: 60.6 us -> 0 us
  other arithmetic: 47.6 us -> 9.09 us
  between operations: 13.4 us -> 0.11 us
    all_gather x4 -> x0, waiting for transfers between devices: 508 us -> none  [the longest x1 350 us: body(): lax.all_gather(w_query, 'fsdp', axis=0, tiled=True)]
    pallas_call x0 -> x1, Pallas kernels: none -> 312 us  [body(): pl.pallas_call(functools.partial(kernel, (n, tps, cores)), out_shape=jax....]
    all_to_all x3 -> x1, waiting for transfers between devices: 158 us -> 0.01 us  [body(): lax.all_to_all(notes, ('fsdp', 'seq'), split_axis=0, concat_axis=0, tiled...]
    dot_general x35 -> x0, matrix products: 85.1 us -> none  [the longest x3 34.9 us: body(): jnp.dot(normed, weight_piece, preferred_element_type=jnp.float32)]
    another operation x2 -> x0, loops' own time: 60.6 us -> none  [the longest x1 60 us: attend(): outputs = lax.map(one_head, jnp.arange(head_total, dtype=jnp.int32))]
    gather x14 -> x2, local copies, waits for them, and re-layouts: 46.8 us -> 9.34 us  [the longest x1 4.93 us: body(): tokens.reshape(block_count, BLOCK, feat)[picked].reshape(rows, feat)]
    reduce_sum x21 -> x5, other arithmetic: 15.3 us -> 3.28 us  [the longest x1 1.15 us: body(): jnp.sum((doc_ids[None, :] < doc_ids[:, None]).astype(jnp.int32), axis=1)]
    neg x2 -> x1, other arithmetic: 11.3 us -> 1.45 us  [body(): sine = jnp.concatenate([-sine, sine], axis=1)]
  transfers between devices with their start and end apart: 7 -> 1, of which waited for: 6 -> 0; matrix products, arithmetic and copies ran while one was open for 7% -> 2% of each run, Pallas kernels for 0% -> 0%
where the time goes in v1:
time: 343 us; the launch traced here: 338 us
  Pallas kernels  312 us (91%)
  local copies, waits for them, and re-layouts  10.7 us (3%)
  other arithmetic  9.09 us (3%)
  starting transfers between devices  6.33 us (2%)
    pallas_call x1, Pallas kernels, body(): pl.pallas_call(functools.partial(kernel, (n, tps, cores)), out_shape=jax....  312 us
  transfers between devices with their start and end apart: 1, of which 0 were waited for; matrix products, arithmetic and copies ran while one was open for 2% of the time, Pallas kernels for 0%

profile of v1, /device:TPU:0, one launch (start us, length us, event | category | flops | bytes accessed | tf_op | source)
XLA Modules:
  0.0 338.2 jit_solution(5790596414860655749)
XLA Ops:
  0.0 0.7 and_select_fusion
  0.7 0.1 reduce_window_sum.11
  0.8 0.2 select_reduce_fusion.2
  1.0 0.2 convert_reduce_fusion.1
  1.2 0.1 add.82
  1.3 1.1 convert_reduce_fusion
  2.4 0.6 all_to_all.8
  3.1 6.3 %all-to-all-start = ((s32[8,1,774]{2,1,0:T(1,128)}), s32[8,1,774]{2,1,0:T(1,128)S(1)}, u32[]{:S(2)}, u32[]{:S(2)}) async-start(s32[8,1,774]{2,1,0:T(1,128)} %all_to_all.8), calls=%async_computation | async-start | bytes 57344 | tf_op jit(solution)/shard_map/all_to_all | solution.py:357
  9.5 0.7 broadcast_add_fusion
  10.3 4.9 %gather_fusion = bf16[48,16,2560]{2,1,0:T(8,128)(2,1)} fusion(bf16[48,16,2560]{2,1,0:T(8,128)(2,1)} %bitcast.14, s32[1024]{0:T(1024)S(1)} %pad_clamp_fusion.1), kind=kCustom, calls=%fused_computation | custom fusion | bytes 7864512 | tf_op jit(solution)/shard_map/gather | solution.py:349
  15.3 0.1 eq.86
  15.4 0.1 fusion.3
  15.5 0.1 mul.90
  15.6 0.1 copy.10
  15.7 0.9 multiply_reduce_fusion.1
  16.6 0.1 convert_element_type.41
  16.7 0.9 multiply_reduce_fusion
  17.6 0.1 eq.89
  17.7 0.1 add.89
  17.8 1.5 fusion
  19.2 1.4 select_convert_fusion.bias_ref
  20.7 1.1 pad_maximum_fusion
  21.8 312.0 %shard_map.91 = bf16[768,2048]{1,0:T(8,128)(2,1)} custom-call(bf16[768,2560]{1,0:T(8,128)(2,1)} %bitcast.15, bf16[1280,2048]{1,0:T(8,128)(2,1)} %wq_ref.1, bf16[1280,256]{1,0:T(8,128)(2,1)} %wk_ref.1, bf16[1280,256]{1,0:T(8,128)(2,1)} %wv_ref.1, f32[1,5120]{1,0:T(1,128)} %bitcast.19, f32[1,128]{1,0:T(1,128)} %bitcast.20, f32[1,128]{1,0:T(1,128)} %bitcast.21, ...), custom_call_target="tpu_custom_call" | custom-call | flops 24964497408 | bytes 26214400 | tf_op jit(solution)/shard_map/pallas_call | solution.py:376
  333.8 4.4 %gather_fusion.1 = bf16[48,16,2048]{2,1,0:T(8,128)(2,1)} fusion(bf16[48,16,2048]{2,1,0:T(8,128)(2,1)} %bitcast.16, s32[1024]{0:T(1024)S(1)} %pad_clamp_fusion), kind=kCustom, calls=%fused_computation.1 | custom fusion | bytes 6291648 | tf_op jit(solution)/shard_map/gather | solution.py:405
  (20 shorter events, 0.4 us)
Async XLA Ops:
  3.1 12.2 %all-to-all-start = ((s32[8,1,774]{2,1,0:T(1,128)}), s32[8,1,774]{2,1,0:T(1,128)S(1)}, u32[]{:S(2)}, u32[]{:S(2)}) async-start(s32[8,1,774]{2,1,0:T(1,128)} %all_to_all.8), calls=%async_computation | async-start | bytes 57344 | tf_op jit(solution)/shard_map/all_to_all | solution.py:357

commit v2 on v1

--- a/solution.py
+++ b/solution.py
@@ -151,14 +151,11 @@
             y_arrival(j, z + step)
 
     def weights(j):
-        z_step(j, 1)
-        if j > 0:
-            y_step(j - 1, n - 1)
-
-        @pl.loop(2, n)
+        @pl.loop(1, n)
         def _(step):
             z_step(j, step)
-            y_step(j, step - 1)
+            if j > 0:
+                y_step(j - 1, step)
 
     def normalise():
         x_local.wait()
@@ -281,13 +278,16 @@
         if j < chunks:
             weights(j)
         else:
-            y_step(chunks - 1, n - 1)
-        if j == 1:
+            @pl.loop(1, n)
+            def _(step):
+                y_step(chunks - 1, step)
+        if j == 3:
             normalise()
-        if j >= 1:
-            ready(j - 1)
-            project(j - 1)
-            dispatch(j - 1)
+        if j >= 3:
+            for k in range(0 if j == 3 else j - 1, j):
+                ready(k)
+                project(k)
+                dispatch(k)
         if j >= 4:
             serve(j - 3)
     for j in range(chunks - 2, chunks):

time: 343 us -> 304 us (0.89)
  Pallas kernels: 312 us -> 275 us
    pallas_call x1, Pallas kernels: 312 us -> 275 us  [body(): pl.pallas_call(functools.partial(kernel, (n, tps, cores)), out_shape=jax....]
where the time goes in v2:
time: 304 us; the launch traced here: 301 us
  Pallas kernels  275 us (90%)
  local copies, waits for them, and re-layouts  10.7 us (4%)
  other arithmetic  9.09 us (3%)
  starting transfers between devices  6.33 us (2%)
    pallas_call x1, Pallas kernels, body(): pl.pallas_call(functools.partial(kernel, (n, tps, cores)), out_shape=jax....  275 us
    all_to_all x1, starting transfers between devices, body(): lax.all_to_all(notes, ('fsdp', 'seq'), split_axis=0, concat_axis=0, tiled...  6.33 us
  transfers between devices with their start and end apart: 1, of which 0 were waited for; matrix products, arithmetic and copies ran while one was open for 2% of the time, Pallas kernels for 0%

profile of v2, /device:TPU:0, one launch (start us, length us, event | category | flops | bytes accessed | tf_op | source)
XLA Modules:
  0.0 300.8 jit_solution(14569607407510155994)
XLA Ops:
  0.0 0.7 and_select_fusion
  0.7 0.1 reduce_window_sum.11
  0.8 0.2 select_reduce_fusion.2
  1.0 0.2 convert_reduce_fusion.1
  1.2 0.1 add.82
  1.3 1.1 convert_reduce_fusion
  2.4 0.6 all_to_all.8
  3.1 6.3 %all-to-all-start = ((s32[8,1,774]{2,1,0:T(1,128)}), s32[8,1,774]{2,1,0:T(1,128)S(1)}, u32[]{:S(2)}, u32[]{:S(2)}) async-start(s32[8,1,774]{2,1,0:T(1,128)} %all_to_all.8), calls=%async_computation | async-start | bytes 57344 | tf_op jit(solution)/shard_map/all_to_all | solution.py:357
  9.5 0.7 broadcast_add_fusion
  10.3 4.9 %gather_fusion = bf16[48,16,2560]{2,1,0:T(8,128)(2,1)} fusion(bf16[48,16,2560]{2,1,0:T(8,128)(2,1)} %bitcast.14, s32[1024]{0:T(1024)S(1)} %pad_clamp_fusion.1), kind=kCustom, calls=%fused_computation | custom fusion | bytes 7864512 | tf_op jit(solution)/shard_map/gather | solution.py:349
  15.3 0.1 eq.86
  15.4 0.1 fusion.3
  15.5 0.1 mul.90
  15.6 0.1 copy.10
  15.7 0.9 multiply_reduce_fusion.1
  16.6 0.1 convert_element_type.41
  16.7 0.9 multiply_reduce_fusion
  17.6 0.1 eq.89
  17.7 0.1 add.89
  17.8 1.5 fusion
  19.2 1.4 select_convert_fusion.bias_ref
  20.7 1.1 pad_maximum_fusion
  21.8 274.6 %shard_map.91 = bf16[768,2048]{1,0:T(8,128)(2,1)} custom-call(bf16[768,2560]{1,0:T(8,128)(2,1)} %bitcast.15, bf16[1280,2048]{1,0:T(8,128)(2,1)} %wq_ref.1, bf16[1280,256]{1,0:T(8,128)(2,1)} %wk_ref.1, bf16[1280,256]{1,0:T(8,128)(2,1)} %wv_ref.1, f32[1,5120]{1,0:T(1,128)} %bitcast.19, f32[1,128]{1,0:T(1,128)} %bitcast.20, f32[1,128]{1,0:T(1,128)} %bitcast.21, ...), custom_call_target="tpu_custom_call" | custom-call | flops 24964497408 | bytes 26214400 | tf_op jit(solution)/shard_map/pallas_call | solution.py:376
  296.4 4.4 %gather_fusion.1 = bf16[48,16,2048]{2,1,0:T(8,128)(2,1)} fusion(bf16[48,16,2048]{2,1,0:T(8,128)(2,1)} %bitcast.16, s32[1024]{0:T(1024)S(1)} %pad_clamp_fusion), kind=kCustom, calls=%fused_computation.1 | custom fusion | bytes 6291648 | tf_op jit(solution)/shard_map/gather | solution.py:405
  (20 shorter events, 0.4 us)
Async XLA Ops:
  3.1 12.2 %all-to-all-start = ((s32[8,1,774]{2,1,0:T(1,128)}), s32[8,1,774]{2,1,0:T(1,128)S(1)}, u32[]{:S(2)}, u32[]{:S(2)}) async-start(s32[8,1,774]{2,1,0:T(1,128)} %all_to_all.8), calls=%async_computation | async-start | bytes 57344 | tf_op jit(solution)/shard_map/all_to_all | solution.py:357
